TPU v7x, 32 devices: a whole 2x2x4 slice. The times are simulated.
32 devices in a mesh: ctx: 8 (over y, x, core), tp: 4 (over z).
Axes of the slice: x: 2, y: 2, z: 4, core: 2. Of those that a mesh axis runs over, the one named last changes fastest.
Arguments:
- rotated_queries: bfloat16 [4096, 8192], P('ctx', 'tp'), may hold values from -25 to 25
- rotated_keys: bfloat16 [4096, 1024], P('ctx', 'tp'), may hold values from -25 to 25
- value_matrix: bfloat16 [4096, 1024], P('ctx', 'tp'), may hold values from -6 to 6
- out_weight: bfloat16 [8192, 8192], P('tp', 'ctx'), may hold values from -0.0625 to 0.0625
- doc_ids: int32 [4096], replicated, may hold values from 0 to 3, never falling along the last dimension, each value on 1 to 2048 neighbouring positions
- assignment: int32 [8, 8], replicated, may hold values from 0 to 7, each once within a row
Outputs:
- owner_output: bfloat16 [4096, 8192], P('ctx', 'tp')
Inputs may be any that keep to these rules, and one draw needn't show every extreme that they name: Each row of assignment is a permutation of 0 to 7. `doc_ids`: documents are numbered in order along the tokens; each has 1 to 2048 tokens and one has exactly 2048.
All inputs are finite; a program needn't handle non-finite values.
Results may differ from a plain program's by a relative error of at most 0.017.
Values may be sent and summed in bfloat16 or wider, within the bound.
A program may use at most 320 MiB of HBM per device.

v0:
```python
import math

import jax
import jax.numpy as jnp
from jax import lax
from jax.sharding import PartitionSpec as P

HEAD_WIDTH = 128


neg_large = -1e30


def refresh(carried, queries_four, query_pos, query_doc, key_part, value_part, key_pos, key_doc):
    running_max, denominator, numerator = carried
    key_count = key_part.shape[0]
    key_tensor_three = key_part.reshape(key_count, -1, HEAD_WIDTH)
    value_tensor_three = value_part.reshape(key_count, -1, HEAD_WIDTH)
    scores = jnp.einsum(
        "tkgd,rkd->tkgr", queries_four, key_tensor_three, preferred_element_type=jnp.float32
    ) * (1.0 / math.sqrt(HEAD_WIDTH))
    visible = (query_doc[:, None] == key_doc[None, :]) & (key_pos[None, :] <= query_pos[:, None])
    visible = visible[:, None, None, :]
    block_max = jnp.max(jnp.where(visible, scores, neg_large), axis=-1)
    new_max = jnp.maximum(running_max, block_max)
    exp_terms = jnp.where(visible, jnp.exp(scores - new_max[..., None]), 0.0)
    denominator = jnp.sum(exp_terms, axis=-1)
    numerator = jnp.einsum(
        "tkgr,rkd->tkgd",
        exp_terms.astype(jnp.bfloat16),
        value_tensor_three,
        preferred_element_type=jnp.float32,
    )
    return (new_max, denominator, numerator)


def attend(local_queries, query_pos, rotated_keys, value_matrix, doc_ids):
    tokens_here = local_queries.shape[0]
    kv_heads = rotated_keys.shape[1] // HEAD_WIDTH
    queries_four = local_queries.reshape(tokens_here, kv_heads, -1, HEAD_WIDTH)
    group_size = queries_four.shape[2]
    query_doc = jnp.take(doc_ids, query_pos)
    initial = (
        jnp.full((tokens_here, kv_heads, group_size), neg_large, jnp.float32),
        jnp.zeros((tokens_here, kv_heads, group_size), jnp.float32),
        jnp.zeros((tokens_here, kv_heads, group_size, HEAD_WIDTH), jnp.float32),
    )
    key_part = lax.all_gather(rotated_keys, "ctx", axis=0, tiled=True)
    value_part = lax.all_gather(value_matrix, "ctx", axis=0, tiled=True)
    key_count = key_part.shape[0]
    key_pos = jnp.arange(key_count, dtype=jnp.int32)
    running_max, denominator, numerator = refresh(
        initial, queries_four, query_pos, query_doc, key_part, value_part, key_pos, doc_ids
    )
    return (numerator / denominator[..., None]).astype(jnp.bfloat16).reshape(tokens_here, -1)


def shards(rotated_queries, rotated_keys, value_matrix, out_weight, doc_ids, assignment):
    owners = lax.axis_size("ctx")
    owner_index = lax.axis_index("ctx")
    tokens_here = rotated_queries.shape[0]
    block_rows = tokens_here // owners
    width = rotated_queries.shape[1]
    my_row = lax.dynamic_index_in_dim(assignment, owner_index, 0, keepdims=False)
    my_column = lax.dynamic_index_in_dim(assignment, owner_index, 1, keepdims=False)
    source_base = jnp.arange(owners, dtype=jnp.int32) * tokens_here
    within_block = jnp.arange(block_rows, dtype=jnp.int32)
    outgoing = jnp.take(rotated_queries.reshape(owners, block_rows, width), my_row, axis=0)
    arrived = lax.all_to_all(outgoing, "ctx", split_axis=0, concat_axis=0, tiled=True)
    owned_pos = (source_base + my_column * block_rows)[:, None] + within_block[None, :]
    attention_output = attend(
        arrived.reshape(tokens_here, width),
        owned_pos.reshape(-1),
        rotated_keys,
        value_matrix,
        doc_ids,
    )
    partial_sums = jnp.dot(
        attention_output,
        lax.all_gather(out_weight, "ctx", axis=1, tiled=True),
        preferred_element_type=jnp.float32,
    )
    return lax.psum_scatter(
        partial_sums.astype(jnp.bfloat16), "tp", scatter_dimension=1, tiled=True
    )


def solution(mesh):
    placed = (P("ctx", "tp"), P("ctx", "tp"), P("ctx", "tp"), P("tp", "ctx"), P(), P())
    return jax.shard_map(
        shards, mesh=mesh, in_specs=placed, out_specs=P("ctx", "tp"), check_vma=False
    )
```

profile of v0, /device:TPU:8, one launch (start us, length us, event | category | flops | bytes accessed | tf_op | source)
XLA Modules:
  0.0 423.3 jit_solution(15092273423209797003)
XLA Ops:
  6.5 0.7 all-gather.6.cloned.1.call-update
  7.3 1.8 copy.8
  9.1 0.0 all-gather.8.cloned.1.call-start
  9.2 0.7 all-gather.8.cloned.1.call-update
  9.9 2.0 gather_fusion.1
  11.9 3.2 broadcast_select_fusion
  15.1 4.4 %all-to-all-start = ((bf16[8,64,2048]{2,1,0:T(8,128)(2,1)}), bf16[8,64,2048]{2,1,0:T(8,128)(2,1)}, u32[]{:S(2)}, u32[]{:S(2)}) async-start(bf16[8,64,2048]{2,1,0:T(8,128)(2,1)} %broadcast_select_fusion), calls=%async_computation | async-start | bytes 4194304 | tf_op jit(solution)/shard_map/all_to_all | solution.py:69
  19.5 0.0 reduce-scatter.2.cloned.1.call-start
  19.5 0.2 add_reduce_fusion
  19.7 0.1 iota_add_fusion
  19.8 0.1 add.94
  19.9 0.1 add.97
  20.0 3.1 gather_fusion
  23.1 2.7 fusion.8
  25.9 26.6 %all-to-all-done = bf16[8,64,2048]{2,1,0:T(8,128)(2,1)} async-done(((bf16[8,64,2048]{2,1,0:T(8,128)(2,1)}), bf16[8,64,2048]{2,1,0:T(8,128)(2,1)}, u32[]{:S(2)}, u32[]{:S(2)}) %all-to-all-start) | async-done | bytes 2097184 | tf_op jit(solution)/shard_map/all_to_all | solution.py:69
  52.5 3.6 copy.16
  56.1 4.1 copy.11
  60.1 23.1 %all-gather.4.cloned.1.call-done = bf16[4096,256]{0,1:T(8,128)(2,1)} async-done(((bf16[512,256]{0,1:T(8,128)(2,1)}), bf16[4096,256]{0,1:T(8,128)(2,1)}) %all-gather.4.cloned.1.call-update) | async-done | bytes 2097168 | tf_op jit(solution)/shard_map/all_gather | solution.py:48
  83.3 54.7 %fusion = (f32[512,2,8]{0,2,1:T(8,128)S(1)}, f32[2,512,8,4096]{3,1,2,0:T(8,128)}) fusion(pred[512,4096]{1,0:T(8,128)(4,1)S(1)} %fusion.8, bf16[4096,2,128,1]{0,2,3,1:T(8,128)(2,1)} %bitcast.51, bf16[512,2,8,128]{3,2,1,0:T(8,128)(2,1)} %bitcast.49), kind=kOutput, calls=%fused_computation.4 | convolution fusion | flops 8690589696 | bytes 140541952 | tf_op jit(solution)/shard_map/tkgd,rkd->tkgr/dot_general | solution.py:19
  137.9 47.2 %fusion.3 = f32[512,2,8]{0,2,1:T(8,128)S(1)} fusion(f32[2,512,8,4096]{3,1,2,0:T(8,128)} %get-tuple-element.6, f32[512,2,8]{0,2,1:T(8,128)S(1)} %broadcast_maximum_fusion, pred[512,4096]{1,0:T(8,128)(4,1)S(1)} %fusion.8), kind=kLoop, calls=%fused_computation.7 | loop fusion | flops 134209536 | bytes 136380416 | tf_op jit(solution)/shard_map/reduce_sum | solution.py:27
  185.1 46.6 %fusion.9 = bf16[512,2,8,128]{0,3,2,1:T(8,128)(2,1)} fusion(bf16[4096,2,128,1]{0,2,3,1:T(8,128)(2,1)} %bitcast.48, f32[2,512,8,4096]{3,1,2,0:T(8,128)} %get-tuple-element.6, f32[512,2,8]{0,2,1:T(8,128)S(1)} %broadcast_maximum_fusion, pred[512,4096]{1,0:T(8,128)(4,1)S(1)} %fusion.8, f32[512,2,8]{0,2,1:T(8,128)S(1)} %fusion.3), kind=kOutput, calls=%fused_computation.15 | convolution fusion | flops 8726249472 | bytes 140574720 | tf_op jit(solution)/shard_map/tkgr,rkd->tkgd/dot_general | solution.py:28
  231.8 14.2 %all-gather.8.cloned.1.call-done = bf16[2048,8192]{1,0:T(8,128)(2,1)} async-done(((bf16[2048,1024]{1,0:T(8,128)(2,1)}), bf16[2048,8192]{1,0:T(8,128)(2,1)}) %all-gather.8.cloned.1.call-update) | async-done | bytes 33554448 | tf_op jit(solution)/shard_map/all_gather | solution.py:80
  246.0 26.4 %convolution_convert_fusion = bf16[512,8192]{1,0:T(8,128)(2,1)} fusion(bf16[512,2048]{0,1:T(8,128)(2,1)} %bitcast.52, bf16[2048,8192]{1,0:T(8,128)(2,1)} %all-gather.8.cloned.1.call-done), kind=kOutput, calls=%fused_computation.11 | convolution fusion | flops 17184063488 | bytes 44040192 | tf_op jit(solution)/shard_map/dot_general | solution.py:78
  272.4 144.3 %reduce-scatter.2.cloned.1.call-done = bf16[512,2048]{1,0:T(8,128)(2,1)} async-done(((bf16[512,8192]{1,0:T(8,128)(2,1)}), bf16[512,2048]{1,0:T(8,128)(2,1)}) %reduce-scatter.2.cloned.1.call-update) | async-done | bytes 2097168 | tf_op jit(solution)/shard_map/reduce_scatter | solution.py:83
  (20 shorter events, 0.1 us)
Async XLA Ops:
  6.5 3.4 copy-start
  6.5 3.3 copy-start.3
  6.5 49.5 %all-gather.6.cloned.1.call-start = ((), (), s32[]{:S(2)}) async-start(), calls=%async_computation.3 | async-start | bytes 2359296 | tf_op jit(solution)/shard_map/all_gather | solution.py:49
  7.3 76.0 %all-gather.4.cloned.1.call-start = ((), (), s32[]{:S(2)}) async-start(), calls=%async_computation.2 | async-start | bytes 2359296 | tf_op jit(solution)/shard_map/all_gather | solution.py:48
  9.1 236.9 %all-gather.8.cloned.1.call-start = ((), (), s32[]{:S(2)}) async-start(), calls=%async_computation.4 | async-start | bytes 37748736 | tf_op jit(solution)/shard_map/all_gather | solution.py:80
  11.9 8.0 %copy-start.2 = (s32[4096]{0:T(1024)S(1)}, s32[4096]{0:T(1024)}, u32[]{:S(2)}) copy-start(s32[4096]{0:T(1024)} %param.10) | copy-start | bytes 49156
  15.1 37.3 %all-to-all-start = ((bf16[8,64,2048]{2,1,0:T(8,128)(2,1)}), bf16[8,64,2048]{2,1,0:T(8,128)(2,1)}, u32[]{:S(2)}, u32[]{:S(2)}) async-start(bf16[8,64,2048]{2,1,0:T(8,128)(2,1)} %broadcast_select_fusion), calls=%async_computation | async-start | bytes 4194304 | tf_op jit(solution)/shard_map/all_to_all | solution.py:69
  19.5 397.3 %reduce-scatter.2.cloned.1.call-start = ((), (), s32[]{:S(2)}) async-start(), calls=%async_computation.5 | async-start | bytes 10485760 | tf_op jit(solution)/shard_map/reduce_scatter | solution.py:83
  272.4 144.3 %copy-start.1 = (bf16[512,2048]{1,0:T(8,128)(2,1)S(1)}, bf16[512,2048]{1,0:T(8,128)(2,1)}, u32[]{:S(2)}) copy-start(bf16[512,2048]{1,0:T(8,128)(2,1)} %param.6) | copy-start | bytes 6291460
Sparse Core Ops, SparseCore 0:
  9.2 41.2 all-gather.5
  52.4 30.7 all-gather.3
  85.2 160.7 all-gather.7
  272.6 144.1 reduce-scatter.1
where the time goes:
time: 426 us; the launch traced here: 423 us
  waiting for transfers between devices  210 us (49%)
  matrix products  128 us (30%)
  other arithmetic  53.4 us (13%)
  local copies, waits for them, and re-layouts  14.8 us (3%)
  between operations  13.2 us (3%)
  starting transfers between devices  4.47 us (1%)
    reduce_scatter x1, waiting for transfers between devices, shards(): lax.psum_scatter(partial_sums.astype(jnp.bfloat16), 'tp', scatter_dimensi...  144 us
    dot_general x1, matrix products, refresh(): jnp.einsum('tkgd,rkd->tkgr', queries_four, key_tensor_three, preferred_el...  54.7 us
    reduce_sum x1, other arithmetic, refresh(): denominator = jnp.sum(exp_terms, axis=-1)  47.2 us
    dot_general x1, matrix products, refresh(): jnp.einsum('tkgr,rkd->tkgd', exp_terms.astype(jnp.bfloat16), value_tensor...  46.6 us
    all_to_all x1, waiting for transfers between devices, shards(): lax.all_to_all(outgoing, 'ctx', split_axis=0, concat_axis=0, tiled=True)  26.6 us
    dot_general x1, matrix products, shards(): jnp.dot(attention_output, lax.all_gather(out_weight, 'ctx', axis=1, tiled...  26.4 us
    all_gather x1, waiting for transfers between devices, attend(): key_part = lax.all_gather(rotated_keys, 'ctx', axis=0, tiled=True)  23.1 us
    all_gather x1, waiting for transfers between devices, shards(): lax.all_gather(out_weight, 'ctx', axis=1, tiled=True)  14.2 us
  transfers between devices with their start and end apart: 5, of which 4 were waited for; matrix products, arithmetic and copies ran while one was open for 40% of the time, Pallas kernels for 0%

commit v1 on v0

v1 whole, which is shorter than its diff:
```python
import functools
import math

import jax
import jax.numpy as jnp
from jax import lax
from jax.experimental import pallas as pl
from jax.experimental.pallas import tpu as pltpu
from jax.sharding import PartitionSpec as P

HEAD_WIDTH = 128
KEY_TILE = 256
QUERY_PER_KV = 8
neg_large = -1e30


def attend_kernel(first, last, q_ref, k_ref, v_ref, start_ref, pos_ref, o_ref):
    block = pl.program_id(1)
    rows = q_ref.shape[0]
    group = q_ref.shape[1] // HEAD_WIDTH
    width = group * rows
    factor = math.log2(math.e) / math.sqrt(HEAD_WIDTH)
    q = jnp.concatenate(
        [q_ref[:, h * HEAD_WIDTH:(h + 1) * HEAD_WIDTH] for h in range(group)], axis=0
    )
    start, pos = start_ref[0], pos_ref[0]

    def tile(i, carried):
        m, total, acc = carried
        base = pl.multiple_of(i * KEY_TILE, KEY_TILE)
        k = k_ref[pl.ds(base, KEY_TILE), :]
        v = v_ref[pl.ds(base, KEY_TILE), :]
        s = lax.dot_general(k, q, (((1,), (1,)), ((), ())), preferred_element_type=jnp.float32)
        key_pos = base + lax.broadcasted_iota(jnp.int32, (KEY_TILE, width), 0)
        s = jnp.where((key_pos >= start) & (key_pos <= pos), s, neg_large)
        new_m = jnp.maximum(m, jnp.max(s, axis=0, keepdims=True))
        alpha = jnp.exp2((m - new_m) * factor)
        p = jnp.exp2((s - new_m) * factor)
        total = total * alpha + jnp.sum(p, axis=0, keepdims=True)
        acc = acc * alpha + lax.dot_general(
            v, p.astype(jnp.bfloat16), (((0,), (0,)), ((), ())), preferred_element_type=jnp.float32
        )
        return new_m, total, acc

    m, total, acc = lax.fori_loop(
        first[block],
        last[block],
        tile,
        (
            jnp.full((1, width), neg_large, jnp.float32),
            jnp.zeros((1, width), jnp.float32),
            jnp.zeros((HEAD_WIDTH, width), jnp.float32),
        ),
    )
    out = (acc / total).T.astype(jnp.bfloat16)
    for h in range(group):
        o_ref[:, h * HEAD_WIDTH:(h + 1) * HEAD_WIDTH] = out[h * rows:(h + 1) * rows]


def attend(queries, block_pos, keys, values, doc_ids, block_rows):
    tokens_here, width = queries.shape
    blocks = tokens_here // block_rows
    kv_heads = keys.shape[1] // HEAD_WIDTH
    group = width // keys.shape[1]
    key_count = keys.shape[0]
    pos = block_pos[:, None] + jnp.arange(block_rows, dtype=jnp.int32)[None, :]
    query_doc = jnp.take(doc_ids, pos)
    start = jnp.sum((doc_ids[None, None, :] < query_doc[:, :, None]).astype(jnp.int32), axis=-1)
    first = start[:, 0] // KEY_TILE
    last = (block_pos + block_rows + KEY_TILE - 1) // KEY_TILE
    start_rows = jnp.tile(start, (1, group))[:, None, :]
    pos_rows = jnp.tile(pos, (1, group))[:, None, :]
    spec = pl.BlockSpec((block_rows, group * HEAD_WIDTH), lambda g, j, *_: (j, g))
    whole = pl.BlockSpec((key_count, HEAD_WIDTH), lambda g, j, *_: (0, g))
    row = pl.BlockSpec((1, 1, group * block_rows), lambda g, j, *_: (j, 0, 0))
    flops = 4 * tokens_here * width * key_count // 4
    return pl.pallas_call(
        attend_kernel,
        out_shape=jax.ShapeDtypeStruct((tokens_here, width), jnp.bfloat16),
        grid_spec=pltpu.PrefetchScalarGridSpec(
            num_scalar_prefetch=2,
            grid=(kv_heads, blocks),
            in_specs=[spec, whole, whole, row, row],
            out_specs=spec,
        ),
        compiler_params=pltpu.CompilerParams(vmem_limit_bytes=32 * 2**20),
        cost_estimate=pl.CostEstimate(
            flops=flops, bytes_accessed=4 * tokens_here * width, transcendentals=flops // 512
        ),
    )(first, last, queries, keys, values, start_rows, pos_rows)


def shards(rotated_queries, rotated_keys, value_matrix, out_weight, doc_ids, assignment):
    owners = lax.axis_size("ctx")
    owner_index = lax.axis_index("ctx")
    tokens_here = rotated_queries.shape[0]
    block_rows = tokens_here // owners
    width = rotated_queries.shape[1]
    my_row = lax.dynamic_index_in_dim(assignment, owner_index, 0, keepdims=False)
    my_column = lax.dynamic_index_in_dim(assignment, owner_index, 1, keepdims=False)
    source_base = jnp.arange(owners, dtype=jnp.int32) * tokens_here
    outgoing = jnp.take(rotated_queries.reshape(owners, block_rows, width), my_row, axis=0)
    arrived = lax.all_to_all(outgoing, "ctx", split_axis=0, concat_axis=0, tiled=True)
    keys = lax.all_gather(rotated_keys, "ctx", axis=0, tiled=True)
    values = lax.all_gather(value_matrix, "ctx", axis=0, tiled=True)
    weight = lax.all_gather(out_weight, "ctx", axis=1, tiled=True)
    attended = attend(
        arrived.reshape(tokens_here, width),
        source_base + my_column * block_rows,
        keys,
        values,
        doc_ids,
        block_rows,
    )
    partial_sums = jnp.dot(attended, weight, preferred_element_type=jnp.float32)
    return lax.psum_scatter(
        partial_sums.astype(jnp.bfloat16), "tp", scatter_dimension=1, tiled=True
    )


def solution(mesh):
    placed = (P("ctx", "tp"), P("ctx", "tp"), P("ctx", "tp"), P("tp", "ctx"), P(), P())
    return jax.shard_map(
        shards, mesh=mesh, in_specs=placed, out_specs=P("ctx", "tp"), check_vma=False
    )
```

time: 426 us -> 425 us (level)
  waiting for transfers between devices: 210 us -> 327 us
  matrix products: 128 us -> 26 us
  other arithmetic: 53.4 us -> 4.55 us
  Pallas kernels: 0 us -> 37.6 us
  local copies, waits for them, and re-layouts: 14.8 us -> 10.1 us
    all_gather x3, waiting for transfers between devices: 37.3 us -> 151 us  [the longest x1 121 us: shards(): weight = lax.all_gather(out_weight, 'ctx', axis=1, tiled=True)]
    dot_general x3 -> x1, matrix products: 128 us -> 26 us  [shards(): partial_sums = jnp.dot(attended, weight, preferred_element_type=jnp.float32)]
    reduce_sum x1, other arithmetic: 47.2 us -> 0.98 us  [attend(): jnp.sum((doc_ids[None, None, :] < query_doc[:, :, None]).astype(jnp.int32...]
    pallas_call x0 -> x1, Pallas kernels: none -> 37.6 us  [attend(): pl.pallas_call(attend_kernel, out_shape=jax.ShapeDtypeStruct((tokens_here...]
  transfers between devices with their start and end apart: 5 -> 5, of which waited for: 4 -> 4; matrix products, arithmetic and copies ran while one was open for 40% -> 2% of each run, Pallas kernels for 0% -> 9%
where the time goes in v1:
time: 425 us; the launch traced here: 423 us
  waiting for transfers between devices  327 us (77%)
  Pallas kernels  37.6 us (9%)
  matrix products  26 us (6%)
  between operations  13.2 us (3%)
  local copies, waits for them, and re-layouts  10.1 us (2%)
  starting transfers between devices  4.61 us (1%)
  other arithmetic  4.55 us (1%)
    reduce_scatter x1, waiting for transfers between devices, shards(): lax.psum_scatter(partial_sums.astype(jnp.bfloat16), 'tp', scatter_dimensi...  144 us
    all_gather x1, waiting for transfers between devices, shards(): weight = lax.all_gather(out_weight, 'ctx', axis=1, tiled=True)  121 us
    pallas_call x1, Pallas kernels, attend(): pl.pallas_call(attend_kernel, out_shape=jax.ShapeDtypeStruct((tokens_here...  37.6 us
    all_gather x1, waiting for transfers between devices, shards(): values = lax.all_gather(value_matrix, 'ctx', axis=0, tiled=True)  30.5 us
    all_to_all x1, waiting for transfers between devices, shards(): lax.all_to_all(outgoing, 'ctx', split_axis=0, concat_axis=0, tiled=True)  28.9 us
    dot_general x1, matrix products, shards(): partial_sums = jnp.dot(attended, weight, preferred_element_type=jnp.float32)  26 us
  transfers between devices with their start and end apart: 5, of which 4 were waited for; matrix products, arithmetic and copies ran while one was open for 2% of the time, Pallas kernels for 9%

profile of v1, /device:TPU:8, one launch (start us, length us, event | category | flops | bytes accessed | tf_op | source)
XLA Modules:
  0.0 422.6 jit_solution(14522012015501511569)
XLA Ops:
  6.5 0.7 all-gather.4.cloned.1.call-update
  7.3 0.7 all-gather.6.cloned.1.call-update
  8.1 0.7 all-gather.8.cloned.1.call-update
  8.8 2.0 gather_fusion.1
  10.8 3.2 broadcast_select_fusion
  14.0 4.5 %all-to-all-start = ((bf16[8,64,2048]{2,1,0:T(8,128)(2,1)}), bf16[8,64,2048]{2,1,0:T(8,128)(2,1)}, u32[]{:S(2)}, u32[]{:S(2)}) async-start(bf16[8,64,2048]{2,1,0:T(8,128)(2,1)} %broadcast_select_fusion), calls=%async_computation | async-start | bytes 4194304 | tf_op jit(solution)/shard_map/all_to_all | solution.py:103
  18.5 0.2 fusion
  18.8 0.1 reshape.164
  18.9 3.1 gather_fusion
  22.1 0.1 reshape.163
  22.1 0.1 iota_add_fusion
  22.2 1.0 convert_reduce_fusion
  23.2 0.1 tile.17.start_ref
  23.3 0.1 tile.19.pos_ref
  23.4 0.1 slice_reduce_fusion
  23.5 28.9 %all-to-all-done = bf16[8,64,2048]{2,1,0:T(8,128)(2,1)} async-done(((bf16[8,64,2048]{2,1,0:T(8,128)(2,1)}), bf16[8,64,2048]{2,1,0:T(8,128)(2,1)}, u32[]{:S(2)}, u32[]{:S(2)}) %all-to-all-start) | async-done | bytes 2097184 | tf_op jit(solution)/shard_map/all_to_all | solution.py:103
  52.5 30.5 %all-gather.6.cloned.1.call-done.v_ref = bf16[4096,256]{1,0:T(8,128)(2,1)} async-done(((bf16[512,256]{1,0:T(8,128)(2,1)}), bf16[4096,256]{1,0:T(8,128)(2,1)}) %all-gather.6.cloned.1.call-update) | async-done | bytes 2097168 | tf_op jit(solution)/shard_map/all_gather | solution.py:105
  83.0 1.6 copy-done.1
  84.6 1.6 copy-done.2
  86.1 37.6 %shard_map.64 = bf16[512,2048]{1,0:T(8,128)(2,1)S(1)} custom-call(s32[8]{0:T(128)S(1)} %get-tuple-element.10.first, s32[8]{0:T(128)S(1)} %get-tuple-element.9.last, bf16[512,2048]{1,0:T(8,128)(2,1)} %bitcast.4.q_ref, bf16[4096,256]{1,0:T(8,128)(2,1)S(1)} %copy-done.1, bf16[4096,256]{1,0:T(8,128)(2,1)S(1)} %copy-done.2, s32[8,1,512]{2,1,0:T(1,128)S(1)} %tile.17.start_ref, ...), custom_call_target="tpu_custom_call" | custom-call | flops 4294967296 | bytes 4194304 | tf_op jit(solution)/shard_map/pallas_call | solution.py:77
  123.7 1.3 copy-done.3
  125.1 120.7 %all-gather.8.cloned.1.call-done = bf16[2048,8192]{1,0:T(8,128)(2,1)} async-done(((bf16[2048,1024]{1,0:T(8,128)(2,1)}), bf16[2048,8192]{1,0:T(8,128)(2,1)}) %all-gather.8.cloned.1.call-update) | async-done | bytes 33554448 | tf_op jit(solution)/shard_map/all_gather | solution.py:106
  245.7 26.0 %convolution_convert_fusion = bf16[512,8192]{1,0:T(8,128)(2,1)} fusion(bf16[512,2048]{1,0:T(8,128)(2,1)} %copy-done.3, bf16[2048,8192]{1,0:T(8,128)(2,1)} %all-gather.8.cloned.1.call-done), kind=kOutput, calls=%fused_computation.2 | convolution fusion | flops 17184063488 | bytes 44040192 | tf_op jit(solution)/shard_map/dot_general | solution.py:115
  271.7 144.3 %reduce-scatter.2.cloned.1.call-done = bf16[512,2048]{1,0:T(8,128)(2,1)} async-done(((bf16[512,8192]{1,0:T(8,128)(2,1)}), bf16[512,2048]{1,0:T(8,128)(2,1)}) %reduce-scatter.2.cloned.1.call-update) | async-done | bytes 2097168 | tf_op jit(solution)/shard_map/reduce_scatter | solution.py:116
  (23 shorter events, 0.3 us)
Async XLA Ops:
  6.5 2.3 copy-start
  6.5 45.9 %all-gather.4.cloned.1.call-start = ((), (), s32[]{:S(2)}) async-start(), calls=%async_computation.2 | async-start | bytes 2359296 | tf_op jit(solution)/shard_map/all_gather | solution.py:104
  7.3 75.7 %all-gather.6.cloned.1.call-start = ((), (), s32[]{:S(2)}) async-start(), calls=%async_computation.3 | async-start | bytes 2359296 | tf_op jit(solution)/shard_map/all_gather | solution.py:105
  8.0 0.8 copy-start.5
  8.0 237.7 %all-gather.8.cloned.1.call-start = ((), (), s32[]{:S(2)}) async-start(), calls=%async_computation.4 | async-start | bytes 37748736 | tf_op jit(solution)/shard_map/all_gather | solution.py:106
  14.0 4.9 %copy-start.4 = (s32[4096]{0:T(1024)S(1)}, s32[4096]{0:T(1024)}, u32[]{:S(2)}) copy-start(s32[4096]{0:T(1024)} %param.10) | copy-start | bytes 49156
  14.0 38.5 %all-to-all-start = ((bf16[8,64,2048]{2,1,0:T(8,128)(2,1)}), bf16[8,64,2048]{2,1,0:T(8,128)(2,1)}, u32[]{:S(2)}, u32[]{:S(2)}) async-start(bf16[8,64,2048]{2,1,0:T(8,128)(2,1)} %broadcast_select_fusion), calls=%async_computation | async-start | bytes 4194304 | tf_op jit(solution)/shard_map/all_to_all | solution.py:103
  18.5 397.6 %reduce-scatter.2.cloned.1.call-start = ((), (), s32[]{:S(2)}) async-start(), calls=%async_computation.5 | async-start | bytes 10485760 | tf_op jit(solution)/shard_map/reduce_scatter | solution.py:116
  83.0 1.6 copy-start.1
  84.5 1.6 copy-start.2
  123.7 1.3 copy-start.3
Sparse Core Ops, SparseCore 0:
  9.2 42.4 all-gather.3
  53.7 29.2 all-gather.5
  84.9 160.8 all-gather.7
  271.9 144.1 reduce-scatter.1

commit v2 on v1

--- a/solution.py
+++ b/solution.py
@@ -10,7 +10,6 @@
 
 HEAD_WIDTH = 128
 KEY_TILE = 256
-QUERY_PER_KV = 8
 neg_large = -1e30
 
 
@@ -57,12 +56,12 @@
         o_ref[:, h * HEAD_WIDTH:(h + 1) * HEAD_WIDTH] = out[h * rows:(h + 1) * rows]
 
 
-def attend(queries, block_pos, keys, values, doc_ids, block_rows):
+def attend(queries, block_pos, keys_values, kv_width, doc_ids, block_rows):
     tokens_here, width = queries.shape
     blocks = tokens_here // block_rows
-    kv_heads = keys.shape[1] // HEAD_WIDTH
-    group = width // keys.shape[1]
-    key_count = keys.shape[0]
+    kv_heads = kv_width // HEAD_WIDTH
+    group = width // kv_width
+    key_count = keys_values.shape[0]
     pos = block_pos[:, None] + jnp.arange(block_rows, dtype=jnp.int32)[None, :]
     query_doc = jnp.take(doc_ids, pos)
     start = jnp.sum((doc_ids[None, None, :] < query_doc[:, :, None]).astype(jnp.int32), axis=-1)
@@ -71,7 +70,8 @@
     start_rows = jnp.tile(start, (1, group))[:, None, :]
     pos_rows = jnp.tile(pos, (1, group))[:, None, :]
     spec = pl.BlockSpec((block_rows, group * HEAD_WIDTH), lambda g, j, *_: (j, g))
-    whole = pl.BlockSpec((key_count, HEAD_WIDTH), lambda g, j, *_: (0, g))
+    key_spec = pl.BlockSpec((key_count, HEAD_WIDTH), lambda g, j, *_: (0, g))
+    value_spec = pl.BlockSpec((key_count, HEAD_WIDTH), lambda g, j, *_: (0, kv_heads + g))
     row = pl.BlockSpec((1, 1, group * block_rows), lambda g, j, *_: (j, 0, 0))
     flops = 4 * tokens_here * width * key_count // 4
     return pl.pallas_call(
@@ -80,42 +80,194 @@
         grid_spec=pltpu.PrefetchScalarGridSpec(
             num_scalar_prefetch=2,
             grid=(kv_heads, blocks),
-            in_specs=[spec, whole, whole, row, row],
+            in_specs=[spec, key_spec, value_spec, row, row],
             out_specs=spec,
         ),
         compiler_params=pltpu.CompilerParams(vmem_limit_bytes=32 * 2**20),
         cost_estimate=pl.CostEstimate(
             flops=flops, bytes_accessed=4 * tokens_here * width, transcendentals=flops // 512
         ),
-    )(first, last, queries, keys, values, start_rows, pos_rows)
+    )(first, last, queries, keys_values, keys_values, start_rows, pos_rows)
+
+
+def project_kernel(n, per, a_ref, w_ref, o_ref, w, acc, own, sent, from_left, from_right,
+                   w_sem, send_sem, left_sem, right_sem):
+    z = lax.axis_index("tp")
+    rows = a_ref.shape[0]
+    tile = min(256, rows)
+    barrier = pltpu.get_barrier_semaphore()
+
+    @pl.when(z > 0)
+    def _():
+        pl.semaphore_signal(barrier, inc=1, device_id={"tp": z - 1}, device_id_type=pl.DeviceIdType.MESH)
+
+    @pl.when(z < n - 1)
+    def _():
+        pl.semaphore_signal(barrier, inc=1, device_id={"tp": z + 1}, device_id_type=pl.DeviceIdType.MESH)
+
+    def fetch(t):
+        piece = pl.ds(t * per, per)
+        return pltpu.make_async_copy(w_ref.at[piece], w.at[piece], w_sem.at[t])
+
+    def rightward(t):
+        return pltpu.make_async_remote_copy(
+            src_ref=sent.at[t], dst_ref=from_left.at[t], send_sem=send_sem.at[t],
+            recv_sem=left_sem.at[t], device_id={"tp": jnp.minimum(z + 1, n - 1)}, device_id_type=pl.DeviceIdType.MESH)
+
+    def leftward(t):
+        return pltpu.make_async_remote_copy(
+            src_ref=sent.at[t], dst_ref=from_right.at[t], send_sem=send_sem.at[t],
+            recv_sem=right_sem.at[t], device_id={"tp": jnp.maximum(z - 1, 0)}, device_id_type=pl.DeviceIdType.MESH)
+
+    def order(k):
+        return lax.select(k % 2 == 0, n - 1 - k // 2, k // 2)
+
+    def begin(k, _):
+        fetch(order(k)).start()
+        return 0
+
+    lax.fori_loop(0, n, begin, 0)
+    pl.semaphore_wait(barrier, (z > 0).astype(jnp.int32) + (z < n - 1).astype(jnp.int32))
+
+    def step(k, _):
+        t = order(k)
+        fetch(t).wait()
+
+        def product(target):
+            def part(r, _):
+                at = pl.ds(pl.multiple_of(r * tile, tile), tile)
+                for i in range(per):
+                    target[i, at, :] = jnp.dot(
+                        a_ref[at, :], w[t * per + i], preferred_element_type=jnp.float32
+                    )
+                return 0
+
+            lax.fori_loop(0, rows // tile, part, 0)
+
+        @pl.when(t == z)
+        def _():
+            product(own)
+
+        @pl.when(t != z)
+        def _():
+            product(acc)
+
+        @pl.when(t > z)
+        def _():
+            @pl.when(z > 0)
+            def _():
+                rightward(t).wait_recv()
+                sent[t] = (acc[...] + from_left[t].astype(jnp.float32)).astype(jnp.bfloat16)
+
+            @pl.when(z == 0)
+            def _():
+                sent[t] = acc[...].astype(jnp.bfloat16)
+
+            rightward(t).start()
+
+        @pl.when(t < z)
+        def _():
+            @pl.when(z < n - 1)
+            def _():
+                leftward(t).wait_recv()
+                sent[t] = (acc[...] + from_right[t].astype(jnp.float32)).astype(jnp.bfloat16)
+
+            @pl.when(z == n - 1)
+            def _():
+                sent[t] = acc[...].astype(jnp.bfloat16)
+
+            leftward(t).start()
+
+        return 0
+
+    lax.fori_loop(0, n, step, 0)
+
+    @pl.when(z > 0)
+    def _():
+        rightward(z).wait_recv()
+        own[...] += from_left[z].astype(jnp.float32)
+
+    @pl.when(z < n - 1)
+    def _():
+        leftward(z).wait_recv()
+        own[...] += from_right[z].astype(jnp.float32)
+
+    o_ref[...] = own[...].astype(jnp.bfloat16)
+
+    def finish(t, _):
+        @pl.when(t > z)
+        def _():
+            rightward(t).wait_send()
+
+        @pl.when(t < z)
+        def _():
+            leftward(t).wait_send()
+
+        return 0
+
+    lax.fori_loop(0, n, finish, 0)
+
+
+def project(attended, weight, n):
+    owners, depth, columns = weight.shape
+    rows = attended.shape[0]
+    per = owners // n
+    slots = pltpu.VMEM((n, per, rows, columns), jnp.bfloat16)
+    sums = pltpu.VMEM((per, rows, columns), jnp.float32)
+    return pl.pallas_call(
+        functools.partial(project_kernel, n, per),
+        out_shape=jax.ShapeDtypeStruct((per, rows, columns), jnp.bfloat16),
+        in_specs=[pl.BlockSpec(memory_space=pltpu.VMEM), pl.BlockSpec(memory_space=pl.ANY)],
+        out_specs=pl.BlockSpec(memory_space=pltpu.VMEM),
+        scratch_shapes=[
+            pltpu.VMEM(weight.shape, jnp.bfloat16), sums, sums, slots, slots, slots,
+        ] + [pltpu.SemaphoreType.DMA((n,))] * 4,
+        compiler_params=pltpu.CompilerParams(
+            collective_id=0, has_side_effects=True, vmem_limit_bytes=48 * 2**20
+        ),
+        cost_estimate=pl.CostEstimate(
+            flops=2 * rows * depth * owners * columns,
+            bytes_accessed=2 * owners * depth * columns,
+            transcendentals=0,
+        ),
+    )(attended, weight)
+
+
+CHUNKS = 4
 
 
 def shards(rotated_queries, rotated_keys, value_matrix, out_weight, doc_ids, assignment):
     owners = lax.axis_size("ctx")
+    tp = lax.axis_size("tp")
     owner_index = lax.axis_index("ctx")
     tokens_here = rotated_queries.shape[0]
     block_rows = tokens_here // owners
     width = rotated_queries.shape[1]
+    kv_width = rotated_keys.shape[1]
     my_row = lax.dynamic_index_in_dim(assignment, owner_index, 0, keepdims=False)
     my_column = lax.dynamic_index_in_dim(assignment, owner_index, 1, keepdims=False)
     source_base = jnp.arange(owners, dtype=jnp.int32) * tokens_here
     outgoing = jnp.take(rotated_queries.reshape(owners, block_rows, width), my_row, axis=0)
     arrived = lax.all_to_all(outgoing, "ctx", split_axis=0, concat_axis=0, tiled=True)
-    keys = lax.all_gather(rotated_keys, "ctx", axis=0, tiled=True)
-    values = lax.all_gather(value_matrix, "ctx", axis=0, tiled=True)
-    weight = lax.all_gather(out_weight, "ctx", axis=1, tiled=True)
+    keys_values = lax.all_gather(
+        jnp.concatenate([rotated_keys, value_matrix], axis=1), "ctx", axis=0, tiled=True
+    )
+    columns = out_weight.shape[1] // CHUNKS
+    weights = [
+        lax.all_gather(out_weight[:, i * columns:(i + 1) * columns], "ctx", axis=0, tiled=False)
+        for i in range(CHUNKS)
+    ]
     attended = attend(
         arrived.reshape(tokens_here, width),
         source_base + my_column * block_rows,
-        keys,
-        values,
+        keys_values,
+        kv_width,
         doc_ids,
         block_rows,
     )
-    partial_sums = jnp.dot(attended, weight, preferred_element_type=jnp.float32)
-    return lax.psum_scatter(
-        partial_sums.astype(jnp.bfloat16), "tp", scatter_dimension=1, tiled=True
-    )
+    parts = [project(attended, weight, tp) for weight in weights]
+    whole = jnp.concatenate(parts, axis=2)
+    return jnp.concatenate([whole[i] for i in range(whole.shape[0])], axis=1)
 
 
 def solution(mesh):

time: 425 us -> 353 us (0.83)
  waiting for transfers between devices: 327 us -> 42.3 us
  Pallas kernels: 37.6 us -> 263 us
  matrix products: 26 us -> 0 us
  local copies, waits for them, and re-layouts: 10.1 us -> 20.7 us
    pallas_call x0 -> x4, Pallas kernels: none -> 217 us  [project(): pl.pallas_call(functools.partial(project_kernel, n, per), out_shape=jax.S...]
    reduce_scatter x1 -> x0, waiting for transfers between devices: 144 us -> none  [shards(): lax.psum_scatter(partial_sums.astype(jnp.bfloat16), 'tp', scatter_dimensi...]
    all_gather x3 -> x5, waiting for transfers between devices: 151 us -> 7.71 us  [the longest x4 7.7 us: shards(): lax.all_gather(out_weight[:, i * columns:(i + 1) * columns], 'ctx', axis=...]
    dot_general x1 -> x0, matrix products: 26 us -> none  [shards(): partial_sums = jnp.dot(attended, weight, preferred_element_type=jnp.float32)]
    pallas_call x1, Pallas kernels: 37.6 us -> 46.1 us  [attend(): pl.pallas_call(attend_kernel, out_shape=jax.ShapeDtypeStruct((tokens_here...]
    unnamed x12 -> x22, local copies, waits for them, and re-layouts: 4.51 us -> 10.7 us
  transfers between devices with their start and end apart: 5 -> 6, of which waited for: 4 -> 3; matrix products, arithmetic and copies ran while one was open for 2% -> 4% of each run, Pallas kernels for 9% -> 60%
where the time goes in v2:
time: 353 us; the launch traced here: 352 us
  Pallas kernels  263 us (75%)
  waiting for transfers between devices  42.3 us (12%)
  local copies, waits for them, and re-layouts  20.7 us (6%)
  between operations  13.3 us (4%)
  other arithmetic  8.49 us (2%)
  starting transfers between devices  4.64 us (1%)
    pallas_call x4, Pallas kernels, project(): pl.pallas_call(functools.partial(project_kernel, n, per), out_shape=jax.S...  217 us
    pallas_call x1, Pallas kernels, attend(): pl.pallas_call(attend_kernel, out_shape=jax.ShapeDtypeStruct((tokens_here...  46.1 us
    all_to_all x1, waiting for transfers between devices, shards(): lax.all_to_all(outgoing, 'ctx', split_axis=0, concat_axis=0, tiled=True)  32.9 us
    unnamed x22, local copies, waits for them, and re-layouts  10.7 us
    all_gather x4, waiting for transfers between devices, shards(): lax.all_gather(out_weight[:, i * columns:(i + 1) * columns], 'ctx', axis=...  7.7 us
  transfers between devices with their start and end apart: 6, of which 3 were waited for; matrix products, arithmetic and copies ran while one was open for 4% of the time, Pallas kernels for 60%

profile of v2, /device:TPU:8, one launch (start us, length us, event | category | flops | bytes accessed | tf_op | source)
XLA Modules:
  0.0 352.1 jit_solution(5709367755168666290)
XLA Ops:
  6.5 2.0 pad_maximum_fusion.2
  8.6 4.2 %fusion.2 = (bf16[2048,256]{1,0:T(8,128)(2,1)}, bf16[2048,256]{1,0:T(8,128)(2,1)}, bf16[2048,256]{1,0:T(8,128)(2,1)}, bf16[2048,256]{1,0:T(8,128)(2,1)}) fusion(bf16[2048,1024]{1,0:T(8,128)(2,1)} %param.9), kind=kLoop, calls=%fused_computation.32 | loop fusion | bytes 8388608 | tf_op jit(solution)/shard_map/slice | solution.py:257
  12.9 0.7 all-gather.14.cloned.1.call-update
  14.2 0.5 all-gather.16.cloned.1.call-update
  14.8 2.0 gather_fusion.1
  16.9 3.3 broadcast_select_fusion
  20.2 4.5 %all-to-all-start = ((bf16[8,64,2048]{2,1,0:T(8,128)(2,1)}), bf16[8,64,2048]{2,1,0:T(8,128)(2,1)}, u32[]{:S(2)}, u32[]{:S(2)}) async-start(bf16[8,64,2048]{2,1,0:T(8,128)(2,1)} %broadcast_select_fusion), calls=%async_computation | async-start | bytes 4194304 | tf_op jit(solution)/shard_map/all_to_all | solution.py:251
  25.0 3.1 gather_fusion
  28.3 1.0 convert_reduce_fusion
  29.6 32.9 %all-to-all-done = bf16[8,64,2048]{2,1,0:T(8,128)(2,1)} async-done(((bf16[8,64,2048]{2,1,0:T(8,128)(2,1)}), bf16[8,64,2048]{2,1,0:T(8,128)(2,1)}, u32[]{:S(2)}, u32[]{:S(2)}) %all-to-all-start) | async-done | bytes 2097184 | tf_op jit(solution)/shard_map/all_to_all | solution.py:251
  62.5 2.2 copy-done.3
  64.7 46.1 %shard_map.64.a_ref = bf16[512,2048]{1,0:T(8,128)(2,1)S(1)} custom-call(s32[8]{0:T(128)S(1)} %get-tuple-element.16.first, s32[8]{0:T(128)S(1)} %get-tuple-element.15.last, bf16[512,2048]{1,0:T(8,128)(2,1)} %bitcast.4.q_ref, bf16[4096,512]{1,0:T(8,128)(2,1)S(1)} %copy-done.3, bf16[4096,512]{1,0:T(8,128)(2,1)S(1)} %copy-done.3, ...), custom_call_target="tpu_custom_call" | custom-call | flops 4294967296 | bytes 4194304 | tf_op jit(solution)/shard_map/pallas_call | solution.py:77
  110.8 1.3 copy-done.4
  112.1 7.6 %all-gather.12.cloned.1.call-done = bf16[16384,256]{1,0:T(8,128)(2,1)} async-done(((bf16[2048,256]{1,0:T(8,128)(2,1)}), bf16[16384,256]{1,0:T(8,128)(2,1)}) %all-gather.12.cloned.1.call-update) | async-done | bytes 8388624 | tf_op jit(solution)/shard_map/all_gather | solution.py:257
  119.7 1.6 copy-done.5
  121.3 54.7 %shard_map.65 = bf16[2,512,256]{2,1,0:T(8,128)(2,1)S(1)} custom-call(bf16[512,2048]{1,0:T(8,128)(2,1)S(1)} %copy-done.5, bf16[8,2048,256]{2,1,0:T(8,128)(2,1)} %bitcast.19), custom_call_target="tpu_custom_call" | custom-call | flops 4294967296 | bytes 8388608 | tf_op jit(solution)/shard_map/pallas_call | solution.py:217
  176.1 1.6 copy-done.6
  177.7 54.7 %shard_map.66 = bf16[2,512,256]{2,1,0:T(8,128)(2,1)S(1)} custom-call(bf16[512,2048]{1,0:T(8,128)(2,1)S(1)} %copy-done.6, bf16[8,2048,256]{2,1,0:T(8,128)(2,1)} %bitcast.20), custom_call_target="tpu_custom_call" | custom-call | flops 4294967296 | bytes 8388608 | tf_op jit(solution)/shard_map/pallas_call | solution.py:217
  232.4 1.6 copy-done.7
  234.0 54.5 %shard_map.68 = bf16[2,512,256]{2,1,0:T(8,128)(2,1)S(1)} custom-call(bf16[512,2048]{1,0:T(8,128)(2,1)S(1)} %copy-done.7, bf16[8,2048,256]{2,1,0:T(8,128)(2,1)} %bitcast.21), custom_call_target="tpu_custom_call" | custom-call | flops 4294967296 | bytes 8388608 | tf_op jit(solution)/shard_map/pallas_call | solution.py:217
  288.5 0.8 copy-done.1
  289.4 1.6 copy-done.8
  291.0 52.7 %shard_map.67 = bf16[2,512,256]{2,1,0:T(8,128)(2,1)S(1)} custom-call(bf16[512,2048]{1,0:T(8,128)(2,1)S(1)} %copy-done.8, bf16[8,2048,256]{2,1,0:T(8,128)(2,1)} %bitcast.22), custom_call_target="tpu_custom_call" | custom-call | flops 4294967296 | bytes 8388608 | tf_op jit(solution)/shard_map/pallas_call | solution.py:217
  344.1 1.5 pad_maximum_fusion.1
  (44 shorter events, 2.1 us)
Async XLA Ops:
  6.5 8.3 %copy-start = (bf16[512,2048]{1,0:T(8,128)(2,1)S(1)}, bf16[512,2048]{1,0:T(8,128)(2,1)}, u32[]{:S(2)}) copy-start(bf16[512,2048]{1,0:T(8,128)(2,1)} %param.6) | copy-start | bytes 6291460
  6.5 56.0 %all-gather.10.cloned.1.call-start = ((), (), s32[]{:S(2)}) async-start(), calls=%async_computation.1 | async-start | bytes 4718592 | tf_op jit(solution)/shard_map/all_gather | solution.py:252
  8.6 111.2 %all-gather.12.cloned.1.call-start = ((), (), s32[]{:S(2)}) async-start(), calls=%async_computation.2 | async-start | bytes 9437184 | tf_op jit(solution)/shard_map/all_gather | solution.py:257
  12.9 1.9 copy-start.10
  12.9 163.2 %all-gather.14.cloned.1.call-start = ((), (), s32[]{:S(2)}) async-start(), calls=%async_computation.3 | async-start | bytes 9437184 | tf_op jit(solution)/shard_map/all_gather | solution.py:257
  13.6 218.7 %all-gather.18.cloned.1.call-start = ((), (), s32[]{:S(2)}) async-start(), calls=%async_computation.5 | async-start | bytes 9437184 | tf_op jit(solution)/shard_map/all_gather | solution.py:257
  14.2 275.2 %all-gather.16.cloned.1.call-start = ((), (), s32[]{:S(2)}) async-start(), calls=%async_computation.4 | async-start | bytes 9437184 | tf_op jit(solution)/shard_map/all_gather | solution.py:257
  20.2 4.8 %copy-start.9 = (s32[4096]{0:T(1024)S(1)}, s32[4096]{0:T(1024)}, u32[]{:S(2)}) copy-start(s32[4096]{0:T(1024)} %param.10) | copy-start | bytes 49156
  20.2 42.3 %all-to-all-start = ((bf16[8,64,2048]{2,1,0:T(8,128)(2,1)}), bf16[8,64,2048]{2,1,0:T(8,128)(2,1)}, u32[]{:S(2)}, u32[]{:S(2)}) async-start(bf16[8,64,2048]{2,1,0:T(8,128)(2,1)} %broadcast_select_fusion), calls=%async_computation | async-start | bytes 4194304 | tf_op jit(solution)/shard_map/all_to_all | solution.py:251
  62.5 2.2 copy-start.3
  110.8 1.3 copy-start.4
  119.7 1.6 copy-start.5
  176.1 1.6 copy-start.6
  232.4 1.6 copy-start.7
  288.5 0.9 copy-start.1
  289.4 1.6 copy-start.8
  290.9 52.7 %copy-start.2 = (bf16[2,512,256]{2,1,0:T(8,128)(2,1)S(1)}, bf16[2,512,256]{2,1,0:T(8,128)(2,1)}, u32[]{:S(2)}) copy-start(bf16[2,512,256]{2,1,0:T(8,128)(2,1)} %copy-done.1) | copy-start | bytes 1572868
Sparse Core Ops, SparseCore 0:
  9.2 49.0 all-gather.9
  60.2 59.4 all-gather.11
  121.6 54.3 all-gather.13
  177.8 54.3 all-gather.17
  234.0 54.3 all-gather.15

commit v3 on v1

--- a/solution.py
+++ b/solution.py
@@ -10,7 +10,6 @@
 
 HEAD_WIDTH = 128
 KEY_TILE = 256
-QUERY_PER_KV = 8
 neg_large = -1e30
 
 
@@ -57,12 +56,12 @@
         o_ref[:, h * HEAD_WIDTH:(h + 1) * HEAD_WIDTH] = out[h * rows:(h + 1) * rows]
 
 
-def attend(queries, block_pos, keys, values, doc_ids, block_rows):
+def attend(queries, block_pos, keys_values, kv_width, doc_ids, block_rows):
     tokens_here, width = queries.shape
     blocks = tokens_here // block_rows
-    kv_heads = keys.shape[1] // HEAD_WIDTH
-    group = width // keys.shape[1]
-    key_count = keys.shape[0]
+    kv_heads = kv_width // HEAD_WIDTH
+    group = width // kv_width
+    key_count = keys_values.shape[0]
     pos = block_pos[:, None] + jnp.arange(block_rows, dtype=jnp.int32)[None, :]
     query_doc = jnp.take(doc_ids, pos)
     start = jnp.sum((doc_ids[None, None, :] < query_doc[:, :, None]).astype(jnp.int32), axis=-1)
@@ -71,7 +70,8 @@
     start_rows = jnp.tile(start, (1, group))[:, None, :]
     pos_rows = jnp.tile(pos, (1, group))[:, None, :]
     spec = pl.BlockSpec((block_rows, group * HEAD_WIDTH), lambda g, j, *_: (j, g))
-    whole = pl.BlockSpec((key_count, HEAD_WIDTH), lambda g, j, *_: (0, g))
+    key_spec = pl.BlockSpec((key_count, HEAD_WIDTH), lambda g, j, *_: (0, g))
+    value_spec = pl.BlockSpec((key_count, HEAD_WIDTH), lambda g, j, *_: (0, kv_heads + g))
     row = pl.BlockSpec((1, 1, group * block_rows), lambda g, j, *_: (j, 0, 0))
     flops = 4 * tokens_here * width * key_count // 4
     return pl.pallas_call(
@@ -80,42 +80,344 @@
         grid_spec=pltpu.PrefetchScalarGridSpec(
             num_scalar_prefetch=2,
             grid=(kv_heads, blocks),
-            in_specs=[spec, whole, whole, row, row],
+            in_specs=[spec, key_spec, value_spec, row, row],
             out_specs=spec,
         ),
         compiler_params=pltpu.CompilerParams(vmem_limit_bytes=32 * 2**20),
         cost_estimate=pl.CostEstimate(
             flops=flops, bytes_accessed=4 * tokens_here * width, transcendentals=flops // 512
         ),
-    )(first, last, queries, keys, values, start_rows, pos_rows)
+    )(first, last, queries, keys_values, keys_values, start_rows, pos_rows)
+
+
+def project_kernel(n, owners, a_ref, first_ref, weight_ref, o_ref, gathered, w, acc, own, sent,
+                   from_left, from_right, w_sem, local_sem, gather_send, gather_recv, send_sem,
+                   left_sem, right_sem):
+    z, me = lax.axis_index("tp"), lax.axis_index("ctx")
+    rows = a_ref.shape[0]
+    columns = weight_ref.shape[1]
+    depth = weight_ref.shape[0]
+    chunks, half = columns // CHUNK, depth // 2
+    per = owners // n
+    tile = min(256, rows)
+    paired = owners == 8
+    twin = me + 1 - 2 * (me % 2)
+    beside = me + 2 - 4 * ((me // 2) % 2)
+    above = me + 4 - 8 * ((me // 4) % 2) if paired else me
+    across = above + 2 - 4 * ((above // 2) % 2)
+    partners = [beside, above, twin] if paired else [(me + i) % owners for i in range(1, owners)]
+
+    barrier = pltpu.get_barrier_semaphore()
+
+    def greet(device):
+        pl.semaphore_signal(barrier, inc=1, device_id=device, device_id_type=pl.DeviceIdType.MESH)
+
+    @pl.when(z > 0)
+    def _():
+        greet({"tp": jnp.maximum(z - 1, 0)})
+
+    @pl.when(z < n - 1)
+    def _():
+        greet({"tp": jnp.minimum(z + 1, n - 1)})
+
+    for partner in partners:
+        greet({"ctx": partner})
+
+    def pass_on(k, owner, piece, target, sid, mine=False):
+        part = pl.ds(0, depth) if piece is None else pl.ds(piece * half, half)
+        if mine:
+            src = weight_ref.at[part, pl.ds(pl.multiple_of(k * CHUNK, CHUNK), CHUNK)]
+        else:
+            src = gathered.at[k, owner, part]
+        return pltpu.make_async_remote_copy(
+            src_ref=src, dst_ref=gathered.at[k, owner, part],
+            send_sem=gather_send.at[k, sid], recv_sem=gather_recv.at[k, owner, piece or 0],
+            device_id={"ctx": target}, device_id_type=pl.DeviceIdType.MESH)
+
+    def keep(k):
+        return pltpu.make_async_copy(
+            weight_ref.at[:, pl.ds(pl.multiple_of(k * CHUNK, CHUNK), CHUNK)],
+            gathered.at[k, me], local_sem.at[k])
+
+    def arrive(k, owner, piece):
+        pass_on(k, owner, piece, partners[0], 0).wait_recv()
+
+    def gather_begin(k):
+        for sid, partner in enumerate(partners):
+            pass_on(k, me, None, partner, sid, mine=True).start()
+        keep(k).start()
+
+    def relay(k, sid):
+        owner, piece, target = {
+            3: (beside, 0, above), 4: (above, 1, beside), 5: (beside, None, twin),
+            6: (above, None, twin), 7: (across, 0, twin), 8: (across, 1, twin),
+        }[sid]
+        return pass_on(k, owner, piece, target, sid)
+
+    def gather_relay(k):
+        if paired:
+            arrive(k, beside, None)
+            relay(k, 3).start()
+            relay(k, 5).start()
+            arrive(k, above, None)
+            relay(k, 4).start()
+            relay(k, 6).start()
+
+    def gather_end(k):
+        if paired:
+            arrive(k, across, 0)
+            relay(k, 7).start()
+            arrive(k, across, 1)
+            relay(k, 8).start()
+            other = [twin]
+            for step in (2, 4):
+                other += [o + step - 2 * step * ((o // step) % 2) for o in other]
+            for owner in other[:3]:
+                arrive(k, owner, None)
+            arrive(k, other[3], 0)
+            arrive(k, other[3], 1)
+        else:
+            for partner in partners:
+                arrive(k, partner, None)
+        keep(k).wait()
+
+    def gather_finish(k):
+        for sid, partner in enumerate(partners):
+            pass_on(k, me, None, partner, sid, mine=True).wait_send()
+        if paired:
+            for sid in range(3, 9):
+                relay(k, sid).wait_send()
+
+    def order(j):
+        return lax.select(j % 2 == 0, n - 1 - j // 2, j // 2)
+
+    def fetch(k, j, source):
+        t, slot = order(j), j % 2
+        return [
+            pltpu.make_async_copy(
+                source.at[k, t * per + i],
+                w.at[slot, :, pl.ds(i * CHUNK, CHUNK)], w_sem.at[slot, i])
+            for i in range(per)
+        ]
+
+    def fetch_start(k, j):
+        @pl.when(k < HEAD)
+        def _():
+            for copy in fetch(jnp.minimum(k, HEAD - 1), j, first_ref):
+                copy.start()
+
+        @pl.when(k >= HEAD)
+        def _():
+            for copy in fetch(k, j, gathered):
+                copy.start()
+
+    def rightward(k, t):
+        return pltpu.make_async_remote_copy(
+            src_ref=sent.at[k, t], dst_ref=from_left.at[k, t], send_sem=send_sem.at[k, t],
+            recv_sem=left_sem.at[k, t], device_id={"tp": jnp.minimum(z + 1, n - 1)},
+            device_id_type=pl.DeviceIdType.MESH)
+
+    def leftward(k, t):
+        return pltpu.make_async_remote_copy(
+            src_ref=sent.at[k, t], dst_ref=from_right.at[k, t], send_sem=send_sem.at[k, t],
+            recv_sem=right_sem.at[k, t], device_id={"tp": jnp.maximum(z - 1, 0)},
+            device_id_type=pl.DeviceIdType.MESH)
+
+    def product(target, slot):
+        def part(r, _):
+            at = pl.ds(pl.multiple_of(r * tile, tile), tile)
+            target[at, :] = jnp.dot(a_ref[at, :], w[slot], preferred_element_type=jnp.float32)
+            return 0
+
+        lax.fori_loop(0, rows // tile, part, 0)
+
+    def reduce_step(k, j):
+        t = order(j)
+
+        @pl.when(j + 1 < n)
+        def _():
+            fetch_start(k, j + 1)
+
+        for copy in fetch(k, j, gathered):
+            copy.wait()
+
+        @pl.when(t == z)
+        def _():
+            product(own, j % 2)
+
+        @pl.when(t != z)
+        def _():
+            product(acc, j % 2)
+
+        @pl.when(t > z)
+        def _():
+            @pl.when(z > 0)
+            def _():
+                rightward(k, t).wait_recv()
+                sent[k, t] = (acc[...] + from_left[k, t].astype(jnp.float32)).astype(jnp.bfloat16)
+
+            @pl.when(z == 0)
+            def _():
+                sent[k, t] = acc[...].astype(jnp.bfloat16)
+
+            rightward(k, t).start()
+
+        @pl.when(t < z)
+        def _():
+            @pl.when(z < n - 1)
+            def _():
+                leftward(k, t).wait_recv()
+                sent[k, t] = (acc[...] + from_right[k, t].astype(jnp.float32)).astype(jnp.bfloat16)
+
+            @pl.when(z == n - 1)
+            def _():
+                sent[k, t] = acc[...].astype(jnp.bfloat16)
+
+            leftward(k, t).start()
+
+    def reduce_end(k):
+        @pl.when(z > 0)
+        def _():
+            rightward(k, z).wait_recv()
+            own[...] += from_left[k, z].astype(jnp.float32)
+
+        @pl.when(z < n - 1)
+        def _():
+            leftward(k, z).wait_recv()
+            own[...] += from_right[k, z].astype(jnp.float32)
+
+        for i in range(per):
+            o_ref[:, pl.ds(pl.multiple_of(i * columns + k * CHUNK, CHUNK), CHUNK)] = own[
+                :, i * CHUNK:(i + 1) * CHUNK
+            ].astype(jnp.bfloat16)
+
+    pl.semaphore_wait(
+        barrier, (z > 0).astype(jnp.int32) + (z < n - 1).astype(jnp.int32) + len(partners)
+    )
+    for k in range(HEAD, min(HEAD + 1, chunks)):
+        gather_begin(k)
+
+    def chunk(k, _):
+        @pl.when((k >= HEAD - 1) & (k + 2 < chunks))
+        def _():
+            gather_begin(k + 2)
+
+        fetch_start(k, 0)
+
+        def step(j, _):
+            reduce_step(k, j)
+            return 0
+
+        lax.fori_loop(0, n, step, 0)
+
+        @pl.when((k + 1 >= HEAD) & (k + 1 < chunks))
+        def _():
+            gather_relay(k + 1)
+
+        reduce_end(k)
+
+        @pl.when((k + 1 >= HEAD) & (k + 1 < chunks))
+        def _():
+            gather_end(k + 1)
+
+        return 0
+
+    lax.fori_loop(0, chunks, chunk, 0)
+
+    def finish(k, _):
+        def one(t, _):
+            @pl.when(t > z)
+            def _():
+                rightward(k, t).wait_send()
+
+            @pl.when(t < z)
+            def _():
+                leftward(k, t).wait_send()
+
+            return 0
+
+        lax.fori_loop(0, n, one, 0)
+
+        @pl.when(k >= HEAD)
+        def _():
+            gather_finish(k)
+
+        return 0
+
+    lax.fori_loop(0, chunks, finish, 0)
+
+
+def project(attended, first, weight, owners, n):
+    rows = attended.shape[0]
+    depth, columns = weight.shape
+    chunks = columns // CHUNK
+    per = owners // n
+    wide = per * CHUNK
+    slots = pltpu.VMEM((chunks, n, rows, wide), jnp.bfloat16)
+    sums = pltpu.VMEM((rows, wide), jnp.float32)
+    dma = pltpu.SemaphoreType.DMA
+    out, _ = pl.pallas_call(
+        functools.partial(project_kernel, n, owners),
+        out_shape=(
+            jax.ShapeDtypeStruct((rows, per * columns), jnp.bfloat16),
+            jax.ShapeDtypeStruct((chunks, owners, depth, CHUNK), jnp.bfloat16),
+        ),
+        in_specs=[
+            pl.BlockSpec(memory_space=pltpu.VMEM),
+            pl.BlockSpec(memory_space=pl.ANY),
+            pl.BlockSpec(memory_space=pl.ANY),
+        ],
+        out_specs=(pl.BlockSpec(memory_space=pltpu.VMEM), pl.BlockSpec(memory_space=pl.ANY)),
+        scratch_shapes=[
+            pltpu.VMEM((2, depth, wide), jnp.bfloat16), sums, sums, slots, slots, slots,
+            dma((2, per)), dma((chunks,)), dma((chunks, max(9, owners))), dma((chunks, owners, 2)),
+            dma((chunks, n)), dma((chunks, n)), dma((chunks, n)),
+        ],
+        compiler_params=pltpu.CompilerParams(
+            collective_id=0, has_side_effects=True, vmem_limit_bytes=48 * 2**20
+        ),
+        cost_estimate=pl.CostEstimate(
+            flops=2 * rows * depth * owners * columns,
+            bytes_accessed=2 * owners * depth * columns,
+            transcendentals=0,
+        ),
+    )(attended, first, weight)
+    return out
+
+
+CHUNK = 128
+HEAD = 1
 
 
 def shards(rotated_queries, rotated_keys, value_matrix, out_weight, doc_ids, assignment):
     owners = lax.axis_size("ctx")
+    tp = lax.axis_size("tp")
     owner_index = lax.axis_index("ctx")
     tokens_here = rotated_queries.shape[0]
     block_rows = tokens_here // owners
     width = rotated_queries.shape[1]
+    kv_width = rotated_keys.shape[1]
     my_row = lax.dynamic_index_in_dim(assignment, owner_index, 0, keepdims=False)
     my_column = lax.dynamic_index_in_dim(assignment, owner_index, 1, keepdims=False)
     source_base = jnp.arange(owners, dtype=jnp.int32) * tokens_here
     outgoing = jnp.take(rotated_queries.reshape(owners, block_rows, width), my_row, axis=0)
     arrived = lax.all_to_all(outgoing, "ctx", split_axis=0, concat_axis=0, tiled=True)
-    keys = lax.all_gather(rotated_keys, "ctx", axis=0, tiled=True)
-    values = lax.all_gather(value_matrix, "ctx", axis=0, tiled=True)
-    weight = lax.all_gather(out_weight, "ctx", axis=1, tiled=True)
+    keys_values = lax.all_gather(
+        jnp.concatenate([rotated_keys, value_matrix], axis=1), "ctx", axis=0, tiled=True
+    )
+    first = jnp.stack([
+        lax.all_gather(out_weight[:, i * CHUNK:(i + 1) * CHUNK], "ctx", axis=0, tiled=False)
+        for i in range(HEAD)
+    ])
     attended = attend(
         arrived.reshape(tokens_here, width),
         source_base + my_column * block_rows,
-        keys,
-        values,
+        keys_values,
+        kv_width,
         doc_ids,
         block_rows,
     )
-    partial_sums = jnp.dot(attended, weight, preferred_element_type=jnp.float32)
-    return lax.psum_scatter(
-        partial_sums.astype(jnp.bfloat16), "tp", scatter_dimension=1, tiled=True
-    )
+    return project(attended, first, out_weight, owners, tp)
 
 
 def solution(mesh):

time: 425 us -> 371 us (0.87)
  waiting for transfers between devices: 327 us -> 37.4 us
  Pallas kernels: 37.6 us -> 291 us
  matrix products: 26 us -> 0 us
    pallas_call x0 -> x1, Pallas kernels: none -> 256 us  [project(): pl.pallas_call(functools.partial(project_kernel, n, owners), out_shape=(j...]
    reduce_scatter x1 -> x0, waiting for transfers between devices: 144 us -> none  [shards(): lax.psum_scatter(partial_sums.astype(jnp.bfloat16), 'tp', scatter_dimensi...]
    all_gather x3 -> x2, waiting for transfers between devices: 151 us -> 7.02 us  [the longest x1 6.35 us: shards(): lax.all_gather(jnp.concatenate([rotated_keys, value_matrix], axis=1), 'ct...]
    dot_general x1 -> x0, matrix products: 26 us -> none  [shards(): partial_sums = jnp.dot(attended, weight, preferred_element_type=jnp.float32)]
  transfers between devices with their start and end apart: 5 -> 3, of which waited for: 4 -> 3; matrix products, arithmetic and copies ran while one was open for 2% -> 3% of each run, Pallas kernels for 9% -> 9%
where the time goes in v3:
time: 371 us; the launch traced here: 367 us
  Pallas kernels  291 us (78%)
  waiting for transfers between devices  37.4 us (10%)
  local copies, waits for them, and re-layouts  13.9 us (4%)
  between operations  13.5 us (4%)
  other arithmetic  6.58 us (2%)
  starting transfers between devices  4.55 us (1%)
    pallas_call x1, Pallas kernels, project(): pl.pallas_call(functools.partial(project_kernel, n, owners), out_shape=(j...  256 us
    pallas_call x1, Pallas kernels, attend(): pl.pallas_call(attend_kernel, out_shape=jax.ShapeDtypeStruct((tokens_here...  34.5 us
    all_to_all x1, waiting for transfers between devices, shards(): lax.all_to_all(outgoing, 'ctx', split_axis=0, concat_axis=0, tiled=True)  30.3 us
  transfers between devices with their start and end apart: 3, of which 3 were waited for; matrix products, arithmetic and copies ran while one was open for 3% of the time, Pallas kernels for 9%

profile of v3, /device:TPU:8, one launch (start us, length us, event | category | flops | bytes accessed | tf_op | source)
XLA Modules:
  0.0 366.5 jit_solution(10561302027788974976)
XLA Ops:
  6.5 2.0 pad_maximum_fusion
  8.7 1.9 slice.7
  10.6 2.0 gather_fusion.1
  12.6 3.2 broadcast_select_fusion
  15.8 4.5 %all-to-all-start = ((bf16[8,64,2048]{2,1,0:T(8,128)(2,1)}), bf16[8,64,2048]{2,1,0:T(8,128)(2,1)}, u32[]{:S(2)}, u32[]{:S(2)}) async-start(bf16[8,64,2048]{2,1,0:T(8,128)(2,1)} %broadcast_select_fusion), calls=%async_computation | async-start | bytes 4194304 | tf_op jit(solution)/shard_map/all_to_all | solution.py:404
  20.3 0.2 fusion
  20.5 0.1 compare_select_fusion
  20.6 0.1 reshape.164
  20.7 3.1 gather_fusion
  23.8 0.1 reshape.163
  23.9 0.1 iota_add_fusion
  24.0 1.0 convert_reduce_fusion
  25.0 0.1 tile.17.start_ref
  25.1 0.1 tile.19.pos_ref
  25.2 0.1 slice_reduce_fusion
  25.3 30.3 %all-to-all-done = bf16[8,64,2048]{2,1,0:T(8,128)(2,1)} async-done(((bf16[8,64,2048]{2,1,0:T(8,128)(2,1)}), bf16[8,64,2048]{2,1,0:T(8,128)(2,1)}, u32[]{:S(2)}, u32[]{:S(2)}) %all-to-all-start) | async-done | bytes 2097184 | tf_op jit(solution)/shard_map/all_to_all | solution.py:404
  55.6 6.3 %all-gather.4.cloned.1.call-done.k_ref.v_ref = bf16[4096,512]{1,0:T(8,128)(2,1)} async-done(((bf16[512,512]{1,0:T(8,128)(2,1)}), bf16[4096,512]{1,0:T(8,128)(2,1)}) %all-gather.4.cloned.1.call-update) | async-done | bytes 4194320 | tf_op jit(solution)/shard_map/all_gather | solution.py:405
  62.0 2.2 copy-done.1
  64.2 34.5 %shard_map.64.a_ref = bf16[512,2048]{1,0:T(8,128)(2,1)S(1)} custom-call(s32[8]{0:T(128)S(1)} %get-tuple-element.12.first, s32[8]{0:T(128)S(1)} %get-tuple-element.11.last, bf16[512,2048]{1,0:T(8,128)(2,1)} %bitcast.4.q_ref, bf16[4096,512]{1,0:T(8,128)(2,1)S(1)} %copy-done.1, bf16[4096,512]{1,0:T(8,128)(2,1)S(1)} %copy-done.1, ...), custom_call_target="tpu_custom_call" | custom-call | flops 4294967296 | bytes 4194304 | tf_op jit(solution)/shard_map/pallas_call | solution.py:77
  98.7 1.3 copy-done.2
  100.0 0.7 all-gather.6.cloned.1.call-done
  100.6 1.6 copy-done.3
  102.2 256.1 %shard_map.65 = (bf16[512,2048]{1,0:T(8,128)(2,1)S(1)}, bf16[8,8,2048,128]{3,2,1,0:T(8,128)(2,1)}) custom-call(bf16[512,2048]{1,0:T(8,128)(2,1)S(1)} %copy-done.3, bf16[1,8,2048,128]{3,2,1,0:T(8,128)(2,1)} %bitcast.12, bf16[2048,1024]{1,0:T(8,128)(2,1)} %weight_ref.1), custom_call_target="tpu_custom_call" | custom-call | flops 17179869184 | bytes 33554432 | tf_op jit(solution)/shard_map/pallas_call | solution.py:359
  358.4 1.3 copy.10
  (20 shorter events, 0.2 us)
Async XLA Ops:
  6.5 4.1 %copy-start = (bf16[512,2048]{1,0:T(8,128)(2,1)S(1)}, bf16[512,2048]{1,0:T(8,128)(2,1)}, u32[]{:S(2)}) copy-start(bf16[512,2048]{1,0:T(8,128)(2,1)} %param.6) | copy-start | bytes 6291460
  6.5 4.0 %copy-start.5 = (s32[8,8]{1,0:T(8,128)S(1)}, s32[8,8]{1,0:T(8,128)}, u32[]{:S(2)}) copy-start(s32[8,8]{1,0:T(8,128)} %param.11) | copy-start | bytes 772
  6.5 55.4 %all-gather.4.cloned.1.call-start = ((), (), s32[]{:S(2)}) async-start(), calls=%async_computation.1 | async-start | bytes 4718592 | tf_op jit(solution)/shard_map/all_gather | solution.py:405
  8.6 92.0 %all-gather.6.cloned.1.call-start = ((), (), s32[]{:S(2)}) async-start(), calls=%async_computation.2 | async-start | bytes 4718592 | tf_op jit(solution)/shard_map/all_gather | solution.py:409
  15.8 4.9 %copy-start.4 = (s32[4096]{0:T(1024)S(1)}, s32[4096]{0:T(1024)}, u32[]{:S(2)}) copy-start(s32[4096]{0:T(1024)} %param.10) | copy-start | bytes 49156
  15.8 39.8 %all-to-all-start = ((bf16[8,64,2048]{2,1,0:T(8,128)(2,1)}), bf16[8,64,2048]{2,1,0:T(8,128)(2,1)}, u32[]{:S(2)}, u32[]{:S(2)}) async-start(bf16[8,64,2048]{2,1,0:T(8,128)(2,1)} %broadcast_select_fusion), calls=%async_computation | async-start | bytes 4194304 | tf_op jit(solution)/shard_map/all_to_all | solution.py:404
  62.0 2.2 copy-start.1
  98.6 1.3 copy-start.2
  100.6 1.6 copy-start.3
Sparse Core Ops, SparseCore 0:
  9.2 52.6 all-gather.3
  63.9 36.7 all-gather.5

commit v4 on v3

--- a/solution.py
+++ b/solution.py
@@ -90,7 +90,7 @@
     )(first, last, queries, keys_values, keys_values, start_rows, pos_rows)
 
 
-def project_kernel(n, owners, a_ref, first_ref, weight_ref, o_ref, gathered, w, acc, own, sent,
+def project_kernel(n, owners, a_ref, first_ref, weight_ref, o_ref, gathered, w, own, sent,
                    from_left, from_right, w_sem, local_sem, gather_send, gather_recv, send_sem,
                    left_sem, right_sem):
     z, me = lax.axis_index("tp"), lax.axis_index("ctx")
@@ -223,15 +223,17 @@
             recv_sem=right_sem.at[k, t], device_id={"tp": jnp.maximum(z - 1, 0)},
             device_id_type=pl.DeviceIdType.MESH)
 
-    def product(target, slot):
+    def product(k, t, slot):
         def part(r, _):
             at = pl.ds(pl.multiple_of(r * tile, tile), tile)
-            target[at, :] = jnp.dot(a_ref[at, :], w[slot], preferred_element_type=jnp.float32)
+            sent[k, t, at, :] = jnp.dot(
+                a_ref[at, :], w[slot], preferred_element_type=jnp.float32
+            ).astype(jnp.bfloat16)
             return 0
 
         lax.fori_loop(0, rows // tile, part, 0)
 
-    def reduce_step(k, j):
+    def multiply(k, j):
         t = order(j)
 
         @pl.when(j + 1 < n)
@@ -240,42 +242,40 @@
 
         for copy in fetch(k, j, gathered):
             copy.wait()
-
-        @pl.when(t == z)
-        def _():
-            product(own, j % 2)
-
-        @pl.when(t != z)
-        def _():
-            product(acc, j % 2)
-
-        @pl.when(t > z)
-        def _():
-            @pl.when(z > 0)
-            def _():
-                rightward(k, t).wait_recv()
-                sent[k, t] = (acc[...] + from_left[k, t].astype(jnp.float32)).astype(jnp.bfloat16)
-
-            @pl.when(z == 0)
-            def _():
-                sent[k, t] = acc[...].astype(jnp.bfloat16)
-
+        product(k, t, j % 2)
+
+        @pl.when((t > z) & (z == 0))
+        def _():
             rightward(k, t).start()
 
-        @pl.when(t < z)
-        def _():
-            @pl.when(z < n - 1)
-            def _():
-                leftward(k, t).wait_recv()
-                sent[k, t] = (acc[...] + from_right[k, t].astype(jnp.float32)).astype(jnp.bfloat16)
-
-            @pl.when(z == n - 1)
-            def _():
-                sent[k, t] = acc[...].astype(jnp.bfloat16)
-
+        @pl.when((t < z) & (z == n - 1))
+        def _():
             leftward(k, t).start()
 
+    def add_on(k, t, other):
+        sent[k, t] = (
+            sent[k, t].astype(jnp.float32) + other[k, t].astype(jnp.float32)
+        ).astype(jnp.bfloat16)
+
+    def forward(i, j):
+        t = order(j)
+        k_right, k_left = i - z, i - (n - 1 - z)
+
+        @pl.when((t > z) & (z > 0) & (k_right >= 0) & (k_right < chunks))
+        def _():
+            rightward(k_right, t).wait_recv()
+            add_on(k_right, t, from_left)
+            rightward(k_right, t).start()
+
+        @pl.when((t < z) & (z < n - 1) & (k_left >= 0) & (k_left < chunks))
+        def _():
+            leftward(k_left, t).wait_recv()
+            add_on(k_left, t, from_right)
+            leftward(k_left, t).start()
+
     def reduce_end(k):
+        own[...] = sent[k, z].astype(jnp.float32)
+
         @pl.when(z > 0)
         def _():
             rightward(k, z).wait_recv()
@@ -297,32 +297,44 @@
     for k in range(HEAD, min(HEAD + 1, chunks)):
         gather_begin(k)
 
-    def chunk(k, _):
-        @pl.when((k >= HEAD - 1) & (k + 2 < chunks))
-        def _():
-            gather_begin(k + 2)
-
-        fetch_start(k, 0)
-
-        def step(j, _):
-            reduce_step(k, j)
+    lag = jnp.maximum(z, n - 1 - z)
+
+    def iteration(i, _):
+        @pl.when((i + 1 >= HEAD) & (i + 1 < chunks))
+        def _():
+            gather_relay(i + 1)
+
+        @pl.when((i >= HEAD - 1) & (i + 2 < chunks))
+        def _():
+            gather_begin(i + 2)
+
+        @pl.when(i < chunks)
+        def _():
+            fetch_start(i, 0)
+
+            def step(j, _):
+                multiply(i, j)
+                return 0
+
+            lax.fori_loop(0, n, step, 0)
+
+        def pass_step(j, _):
+            forward(i, j)
             return 0
 
-        lax.fori_loop(0, n, step, 0)
-
-        @pl.when((k + 1 >= HEAD) & (k + 1 < chunks))
-        def _():
-            gather_relay(k + 1)
-
-        reduce_end(k)
-
-        @pl.when((k + 1 >= HEAD) & (k + 1 < chunks))
-        def _():
-            gather_end(k + 1)
+        lax.fori_loop(0, n, pass_step, 0)
+
+        @pl.when((i + 1 >= HEAD) & (i + 1 < chunks))
+        def _():
+            gather_end(i + 1)
+
+        @pl.when((i >= lag) & (i - lag < chunks))
+        def _():
+            reduce_end(i - lag)
 
         return 0
 
-    lax.fori_loop(0, chunks, chunk, 0)
+    lax.fori_loop(0, chunks + n - 1, iteration, 0)
 
     def finish(k, _):
         def one(t, _):
@@ -369,7 +381,7 @@
         ],
         out_specs=(pl.BlockSpec(memory_space=pltpu.VMEM), pl.BlockSpec(memory_space=pl.ANY)),
         scratch_shapes=[
-            pltpu.VMEM((2, depth, wide), jnp.bfloat16), sums, sums, slots, slots, slots,
+            pltpu.VMEM((2, depth, wide), jnp.bfloat16), sums, slots, slots, slots,
             dma((2, per)), dma((chunks,)), dma((chunks, max(9, owners))), dma((chunks, owners, 2)),
             dma((chunks, n)), dma((chunks, n)), dma((chunks, n)),
         ],
@@ -385,7 +397,7 @@
     return out
 
 
-CHUNK = 128
+CHUNK = 256
 HEAD = 1
 
 

time: 371 us -> 311 us (0.84); the launches traced: 367 us -> 311 us
  Pallas kernels: 291 us -> 211 us
  waiting for transfers between devices: 37.4 us -> 60.2 us
    pallas_call x1, Pallas kernels: 256 us -> 181 us  [project(): pl.pallas_call(functools.partial(project_kernel, n, owners), out_shape=(j...]
    all_gather x1, waiting for transfers between devices: 0.67 us -> 23.1 us  [shards(): lax.all_gather(out_weight[:, i * CHUNK:(i + 1) * CHUNK], 'ctx', axis=0, t...]
    pallas_call x1, Pallas kernels: 34.5 us -> 29.7 us  [attend(): pl.pallas_call(attend_kernel, out_shape=jax.ShapeDtypeStruct((tokens_here...]
    unnamed x13 -> x15, local copies, waits for them, and re-layouts: 6.42 us -> 7.45 us
  transfers between devices with their start and end apart: 3 -> 3, of which waited for: 3 -> 3; matrix products, arithmetic and copies ran while one was open for 3% -> 4% of each run, Pallas kernels for 9% -> 10%
where the time goes in v4:
time: 311 us
  Pallas kernels  211 us (68%)
  waiting for transfers between devices  60.2 us (19%)
  local copies, waits for them, and re-layouts  15.3 us (5%)
  between operations  13.5 us (4%)
  other arithmetic  6.57 us (2%)
  starting transfers between devices  3.9 us (1%)
    pallas_call x1, Pallas kernels, project(): pl.pallas_call(functools.partial(project_kernel, n, owners), out_shape=(j...  181 us
    all_to_all x1, waiting for transfers between devices, shards(): lax.all_to_all(outgoing, 'ctx', split_axis=0, concat_axis=0, tiled=True)  30.4 us
    pallas_call x1, Pallas kernels, attend(): pl.pallas_call(attend_kernel, out_shape=jax.ShapeDtypeStruct((tokens_here...  29.7 us
    all_gather x1, waiting for transfers between devices, shards(): lax.all_gather(out_weight[:, i * CHUNK:(i + 1) * CHUNK], 'ctx', axis=0, t...  23.1 us
    unnamed x15, local copies, waits for them, and re-layouts  7.45 us
    all_gather x1, waiting for transfers between devices, shards(): lax.all_gather(jnp.concatenate([rotated_keys, value_matrix], axis=1), 'ct...  6.63 us
  transfers between devices with their start and end apart: 3, of which 3 were waited for; matrix products, arithmetic and copies ran while one was open for 4% of the time, Pallas kernels for 10%

profile of v4, /device:TPU:8, one launch (start us, length us, event | category | flops | bytes accessed | tf_op | source)
XLA Modules:
  0.0 310.7 jit_solution(4693541495698316687)
XLA Ops:
  6.5 2.0 pad_maximum_fusion
  8.6 2.3 slice.7
  11.0 2.0 gather_fusion.1
  13.0 3.2 %broadcast_select_fusion = bf16[8,64,2048]{2,1,0:T(8,128)(2,1)} fusion(bf16[8,64,2048]{2,1,0:T(8,128)(2,1)} %gather_fusion.1, pred[8]{0:T(512)(128)(4,1)S(1)} %compare_and_fusion), kind=kLoop, calls=%fused_computation.3 | loop fusion | flops 1048576 | bytes 4194312 | tf_op jit(solution)/shard_map/jit(_take)/select_n | solution.py:415
  16.2 3.9 %all-to-all-start = ((bf16[8,64,2048]{2,1,0:T(8,128)(2,1)}), bf16[8,64,2048]{2,1,0:T(8,128)(2,1)S(1)}, u32[]{:S(2)}, u32[]{:S(2)}) async-start(bf16[8,64,2048]{2,1,0:T(8,128)(2,1)} %broadcast_select_fusion), calls=%async_computation | async-start | bytes 4194304 | tf_op jit(solution)/shard_map/all_to_all | solution.py:416
  20.0 0.2 fusion
  20.3 0.1 reshape.164
  20.4 3.1 %gather_fusion = s32[512]{0:T(512)S(1)} fusion(s32[4096]{0:T(1024)S(1)} %copy-done.5, s32[1024]{0:T(1024)S(1)} %pad_clamp_fusion.1), kind=kCustom, calls=%fused_computation | custom fusion | bytes 6144 | tf_op jit(solution)/shard_map/jit(_take)/gather | solution.py:66
  23.5 0.1 reshape.163
  23.6 0.1 iota_add_fusion
  23.7 1.0 convert_reduce_fusion
  24.7 0.1 tile.17.start_ref
  24.8 0.1 tile.19.pos_ref
  24.9 0.1 slice_reduce_fusion
  25.0 30.4 %all-to-all-done = bf16[8,64,2048]{2,1,0:T(8,128)(2,1)S(1)} async-done(((bf16[8,64,2048]{2,1,0:T(8,128)(2,1)}), bf16[8,64,2048]{2,1,0:T(8,128)(2,1)S(1)}, u32[]{:S(2)}, u32[]{:S(2)}) %all-to-all-start) | async-done | bytes 2097184 | tf_op jit(solution)/shard_map/all_to_all | solution.py:416
  55.4 6.6 %all-gather.4.cloned.1.call-done.k_ref.v_ref = bf16[4096,512]{1,0:T(8,128)(2,1)} async-done(((bf16[512,512]{1,0:T(8,128)(2,1)}), bf16[4096,512]{1,0:T(8,128)(2,1)}) %all-gather.4.cloned.1.call-update) | async-done | bytes 4194320 | tf_op jit(solution)/shard_map/all_gather | solution.py:417
  62.0 2.2 copy-done.2
  64.2 29.7 %shard_map.64.a_ref = bf16[512,2048]{1,0:T(8,128)(2,1)S(1)} custom-call(s32[8]{0:T(128)S(1)} %get-tuple-element.12.first, s32[8]{0:T(128)S(1)} %get-tuple-element.11.last, bf16[512,2048]{1,0:T(8,128)(2,1)S(1)} %bitcast.12, bf16[4096,512]{1,0:T(8,128)(2,1)S(1)} %copy-done.2, bf16[4096,512]{1,0:T(8,128)(2,1)S(1)} %copy-done.2, ...), custom_call_target="tpu_custom_call" | custom-call | flops 4294967296 | bytes 4194304 | tf_op jit(solution)/shard_map/pallas_call | solution.py:77
  93.9 1.3 copy-done.3
  95.2 23.1 %all-gather.6.cloned.1.call-done = bf16[16384,256]{1,0:T(8,128)(2,1)} async-done(((bf16[2048,256]{1,0:T(8,128)(2,1)}), bf16[16384,256]{1,0:T(8,128)(2,1)}) %all-gather.6.cloned.1.call-update) | async-done | bytes 8388624 | tf_op jit(solution)/shard_map/all_gather | solution.py:421
  118.4 1.6 copy-done.4
  120.0 181.5 %shard_map.65 = (bf16[512,2048]{1,0:T(8,128)(2,1)S(1)}, bf16[4,8,2048,256]{3,2,1,0:T(8,128)(2,1)}) custom-call(bf16[512,2048]{1,0:T(8,128)(2,1)S(1)} %copy-done.4, bf16[1,8,2048,256]{3,2,1,0:T(8,128)(2,1)} %bitcast.13, bf16[2048,1024]{1,0:T(8,128)(2,1)} %weight_ref.1), custom_call_target="tpu_custom_call" | custom-call | flops 17179869184 | bytes 33554432 | tf_op jit(solution)/shard_map/pallas_call | solution.py:371
  301.5 1.3 copy.10
  302.8 1.0 copy-done.1
  (22 shorter events, 0.2 us)
Async XLA Ops:
  6.5 4.4 %copy-start = (bf16[512,2048]{1,0:T(8,128)(2,1)S(1)}, bf16[512,2048]{1,0:T(8,128)(2,1)}, u32[]{:S(2)}) copy-start(bf16[512,2048]{1,0:T(8,128)(2,1)} %param.6) | copy-start | bytes 6291460
  6.5 55.4 %all-gather.4.cloned.1.call-start = ((), (), s32[]{:S(2)}) async-start(), calls=%async_computation.1 | async-start | bytes 4718592 | tf_op jit(solution)/shard_map/all_gather | solution.py:417
  8.6 2.4 copy-start.6
  8.6 109.8 %all-gather.6.cloned.1.call-start = ((), (), s32[]{:S(2)}) async-start(), calls=%async_computation.2 | async-start | bytes 9437184 | tf_op jit(solution)/shard_map/all_gather | solution.py:421
  16.2 4.2 %copy-start.5 = (s32[4096]{0:T(1024)S(1)}, s32[4096]{0:T(1024)}, u32[]{:S(2)}) copy-start(s32[4096]{0:T(1024)} %param.10) | copy-start | bytes 49156
  16.2 39.2 %all-to-all-start = ((bf16[8,64,2048]{2,1,0:T(8,128)(2,1)}), bf16[8,64,2048]{2,1,0:T(8,128)(2,1)S(1)}, u32[]{:S(2)}, u32[]{:S(2)}) async-start(bf16[8,64,2048]{2,1,0:T(8,128)(2,1)} %broadcast_select_fusion), calls=%async_computation | async-start | bytes 4194304 | tf_op jit(solution)/shard_map/all_to_all | solution.py:416
  62.0 2.2 copy-start.2
  93.9 1.3 copy-start.3
  118.4 1.6 copy-start.4
  301.5 2.4 copy-start.1
Sparse Core Ops, SparseCore 0:
  9.2 52.6 all-gather.3
  63.9 54.4 all-gather.5
